TPU v7x, 128 devices: a whole 4x4x4 slice. The times are simulated.
128 devices in a mesh: tx: 8 (over y, core), ty: 16 (over z, x).
Axes of the slice: x: 4, y: 4, z: 4, core: 2. Of those that a mesh axis runs over, the one named last changes fastest.
Arguments:
- probes: bfloat16 [512, 64, 2048], P(('tx', 'ty')), may hold values from -6 to 6
- points: float32 [512, 8, 2048], P(('tx', 'ty')), may hold values from 0 to 1
- up_basis: bfloat16 [512, 256, 2048], P(('tx', 'ty')), may hold values from -0.125 to 0.125
- down_basis: bfloat16 [512, 256, 2048], P(('tx', 'ty')), may hold values from -0.09375 to 0.09375
- box_skeleton: int32 [512, 256], P(('tx', 'ty')), may hold values from 0 to 2047, as said below
- box_transfer: bfloat16 [512, 256, 256], P(('tx', 'ty')), may hold values from -0.375 to 0.375
- node_skeleton: int32 [128, 256], P(('tx', 'ty')), may hold values from 0 to 1023, as said below
- node_transfer: bfloat16 [128, 256, 256], P(('tx', 'ty')), may hold values from -0.375 to 0.375
- group_skeleton: int32 [8, 256], replicated, may hold values from 0 to 4095, as said below
- near_list: int32 [512, 3], P(('tx', 'ty')), may hold values from -1 to 511, as said below
- node_list: int32 [128, 8], P(('tx', 'ty')), may hold values from 0 to 127, as said below
Outputs:
- applied: bfloat16 [512, 64, 2048], P(('tx', 'ty'))
Inputs may be any that keep to these rules, and one draw needn't show every extreme that they name: `box_skeleton`: each row names 256 distinct points of its box. `node_skeleton`: each row names 256 distinct points among the 1024 skeleton points of the node's boxes, numbered box by box. `group_skeleton`: each row names 256 distinct points among the 4096 skeleton points of the group's middle-level nodes, numbered node by node. `near_list`: box b of node d names 1 to 3 distinct boxes, live entries first and -1 after them; every named box belongs to d or to the nodes d - 1 and d + 1 where these lie in d's upper-level node. `node_list`: node d names 8 distinct nodes of its own upper-level node whose ty index differs from d's by two or more.
All inputs are finite; a program needn't handle non-finite values.
Results may differ from a plain program's by a relative error of at most 0.024.
Values may be sent and summed in bfloat16 or wider, within the bound.
No kernel may reach another device: no remote copies, remote signals or barrier semaphores. Data moves between devices by JAX's collectives and lax.ppermute only.
A program may use at most 128 MiB of HBM per device.

v0:
```python
import functools
import math

import jax
import jax.numpy as jnp
from jax import lax
from jax.experimental import pallas as pl
from jax.experimental.pallas import tpu as pltpu
from jax.sharding import PartitionSpec as P

bf16 = jnp.bfloat16
f32 = jnp.float32
i32 = jnp.int32

INV_LENGTH = 4.0
LN2 = math.log(2.0)
SCALE = INV_LENGTH / LN2
VMEM = pl.BlockSpec(memory_space=pltpu.VMEM)
SMEM = pl.BlockSpec(memory_space=pltpu.SMEM)
TILE_ROWS = 1024
TILE_COLS = 256
OWN_UNITS = 4
LATE_UNITS = 7
FIRST_LATE = 3
GROUP_ROWS = 256
LAST_AT = OWN_UNITS + LATE_UNITS
LAST_UNITS = 7
COLUMNS = LAST_AT + LAST_UNITS
SIDE, BOX, LIVE, OPENS, CLOSES, PREV, OWN, NEXT = range(8)


def params(mib=62):
    return pltpu.CompilerParams(vmem_limit_bytes=mib * 2**20)


SMALL = pl.CostEstimate(flops=1024, bytes_accessed=1024, transcendentals=0)


def split_points(points):
    scaled = (points - 0.5) * SCALE
    high = scaled.astype(bf16)
    low = (scaled - high.astype(f32)).astype(bf16)
    return high, low


def norm_rows(pair, one_first):
    high = pair[:8]
    low = pair[8:]
    full = high + low
    norm = jnp.sum(full * full, axis=0, keepdims=True)
    first = norm.astype(bf16).astype(f32)
    rest = norm - first
    second = rest.astype(bf16).astype(f32)
    third = rest - second
    row = lax.broadcasted_iota(i32, high.shape, 0)
    base = 3 if one_first else 0
    ones = 0 if one_first else 3
    out = jnp.where((row >= ones) & (row < ones + 3), 1.0, 0.0)
    out = jnp.where(row == base, first, out)
    out = jnp.where(row == base + 1, second, out)
    return jnp.where(row == base + 2, third, out)


def source_features(pair):
    high = pair[:8] * -2.0
    low = pair[8:] * -2.0
    return jnp.concatenate([high, low, high, norm_rows(pair, False)], axis=0).T.astype(bf16)


def target_features(pair):
    high = pair[:8]
    return jnp.concatenate([high, high, pair[8:], norm_rows(pair, True)], axis=0).astype(bf16)


def entries(squared):
    squared = jnp.maximum(squared, 1e-12)
    scaled = squared * lax.rsqrt(squared)
    return (scaled * jnp.exp2(-scaled)).astype(bf16)


def dot(a, b):
    return jnp.dot(a, b, preferred_element_type=f32)


def dot_nt(a, b):
    return lax.dot_general(a, b, (((1,), (1,)), ((), ())), preferred_element_type=f32)


def write_table(near_ref, base_ref, table_ref):
    boxes, width = near_ref.shape
    for column in range(COLUMNS):
        table_ref[SIDE, column] = i32(1)
        table_ref[BOX, column] = i32(boxes - 1)
        for row in (LIVE, OPENS, CLOSES, PREV, OWN, NEXT):
            table_ref[row, column] = i32(0)

    units = []
    for box in range(boxes):
        for entry in range(width):
            named = near_ref[box, entry]
            slot = jnp.clip(named - base_ref[0], 0, 3 * boxes - 1)
            side = (slot >= boxes).astype(i32) + (slot >= 2 * boxes).astype(i32)
            units.append((box, named >= 0, side, slot - side * boxes))

    def put(column, when, box, side, index, hold):
        hold = [jnp.where(when & (side == k), index, hold[k]) for k in range(3)]

        @pl.when(when)
        def _():
            table_ref[SIDE, column] = side
            table_ref[BOX, column] = i32(box)
            table_ref[LIVE, column] = i32(1)
            for k, row in enumerate((PREV, OWN, NEXT)):
                table_ref[row, column] = hold[k]

        return hold

    zero = i32(0)
    own_rank = zero
    rest_rank = zero
    last_column = i32(LAST_AT)
    own_hold, late_hold, last_hold = [zero] * 3, [zero] * 3, [zero] * 3
    for box in range(boxes):
        opened = last_column
        for _, live, side, index in units[box * width : (box + 1) * width]:
            early = live & (side == 1) & (own_rank < OWN_UNITS)
            own_hold = put(own_rank, early, box, side, index, own_hold)
            own_rank = own_rank + early.astype(i32)
            rest = live & jnp.logical_not(early)
            late = rest & (rest_rank < LATE_UNITS)
            late_hold = put(OWN_UNITS + rest_rank, late, box, side, index, late_hold)
            rest_rank = rest_rank + rest.astype(i32)
            last = rest & jnp.logical_not(late)
            last_hold = put(last_column, last, box, side, index, last_hold)
            last_column = last_column + last.astype(i32)
        bare = last_column == opened

        @pl.when(bare)
        def _(column=last_column, box=box, hold=tuple(last_hold)):
            table_ref[BOX, column] = i32(box)
            for k, row in enumerate((PREV, OWN, NEXT)):
                table_ref[row, column] = hold[k]

        last_column = last_column + bare.astype(i32)
        table_ref[OPENS, opened] = i32(1)
        table_ref[CLOSES, last_column - 1] = i32(1)


def one_hot(index_row, size, offset=0):
    rows = lax.broadcasted_iota(i32, (size, index_row.shape[1]), 0) + offset
    return jnp.where(rows == index_row, 1.0, 0.0).astype(bf16)


def prep_kernel(
    near_ref,
    base_ref,
    probes_ref,
    points_ref,
    up_ref,
    box_skel_ref,
    transfer_ref,
    node_skel_ref,
    node_transfer_ref,
    packed_ref,
    table_ref,
    out_ref,
    acc,
    pool,
):
    b = pl.program_id(0)
    boxes = pl.num_programs(0)
    rank = up_ref.shape[1]
    leaf = up_ref.shape[2]

    @pl.when(b == 0)
    def _():
        write_table(near_ref, base_ref, table_ref)
        acc[...] = jnp.zeros_like(acc)

    packed_ref[0, :64, :] = probes_ref[0]
    high, low = split_points(points_ref[0])
    pair = jnp.concatenate([high.astype(f32), low.astype(f32)], axis=0).astype(bf16)
    packed_ref[0, 64:80, :] = pair
    weights = dot_nt(probes_ref[0], up_ref[0]).astype(bf16)
    acc[...] += dot(weights, transfer_ref[0])
    pool[b] = dot(pair, one_hot(box_skel_ref[pl.ds(b, 1), :], leaf)).astype(bf16)

    @pl.when(b == boxes - 1)
    def _():
        node_weight = acc[...].astype(bf16)
        out_ref[0:64, :] = node_weight
        found = jnp.zeros((16, rank), f32)
        for k in range(pool.shape[0]):
            found = found + dot(pool[k], one_hot(node_skel_ref[...], rank, k * rank))
        out_ref[64:80, :] = found.astype(bf16)
        out_ref[80:144, :] = dot(node_weight, node_transfer_ref[0]).astype(bf16)


def prep(near_list, base, probes, points, up_basis, box_skeleton, box_transfer, node_skeleton, node_transfer):
    boxes, count, leaf = probes.shape
    rank = up_basis.shape[1]

    def by_box(shape):
        return pl.BlockSpec((1,) + shape, lambda b: (b, 0, 0))

    def whole(shape):
        return pl.BlockSpec(shape, lambda b: (0,) * len(shape))

    return pl.pallas_call(
        prep_kernel,
        grid=(boxes,),
        in_specs=[
            SMEM,
            SMEM,
            by_box((count, leaf)),
            by_box((8, leaf)),
            by_box((rank, leaf)),
            whole((boxes, rank)),
            by_box((rank, rank)),
            whole((1, rank)),
            whole((1, rank, rank)),
        ],
        out_specs=[by_box((count + 16, leaf)), SMEM, whole((144, rank))],
        out_shape=[
            jax.ShapeDtypeStruct((boxes, count + 16, leaf), bf16),
            jax.ShapeDtypeStruct((8, COLUMNS), i32),
            jax.ShapeDtypeStruct((144, rank), bf16),
        ],
        scratch_shapes=[pltpu.VMEM((64, rank), f32), pltpu.VMEM((boxes, 16, rank), bf16)],
        compiler_params=params(),
        name="prep",
    )(near_list, base, probes, points, up_basis, box_skeleton, box_transfer, node_skeleton, node_transfer)


def load_source(table, column, sources, held, left):
    side = table[SIDE, column]
    for k, ref in sources:

        @pl.when(side == k)
        def _(ref=ref):
            held[...] = ref[0, :64, :]
            left[...] = source_features(ref[0, 64:80, :].astype(f32))


def near_tile(held, left, right, write):
    leaf = left.shape[0]
    steps = leaf // TILE_ROWS
    for j in range(leaf // TILE_COLS):
        cols = slice(j * TILE_COLS, (j + 1) * TILE_COLS)
        total = None
        block = None
        ahead = dot(left[0:TILE_ROWS, :], right[:, cols])
        for k in range(steps):
            squared = ahead
            if k + 1 < steps:
                ahead = dot(left[(k + 1) * TILE_ROWS : (k + 2) * TILE_ROWS, :], right[:, cols])
            before, block = block, entries(squared)
            if before is not None:
                term = dot(held[:, (k - 1) * TILE_ROWS : k * TILE_ROWS], before)
                total = term if total is None else total + term
        term = dot(held[:, (steps - 1) * TILE_ROWS :], block)
        write(cols, term if total is None else total + term)


def early_kernel(start, sides, table, *refs):
    sources = refs[: len(sides)]
    target_ref, out_ref, held, left, right = refs[len(sides) :]
    column = pl.program_id(0) + start

    @pl.when(table[LIVE, column] == 1)
    def _():
        load_source(table, column, list(zip(sides, sources)), held, left)
        right[...] = target_features(target_ref[0].astype(f32))

        def write(cols, total):
            out_ref[0, :, cols] = total

        near_tile(held, left, right, write)


def source_specs(start, sides, rows, leaf):
    def spec(row):
        return pl.BlockSpec((1, rows, leaf), lambda i, table: (table[row, i + start], 0, 0))

    target = pl.BlockSpec((1, 16, leaf), lambda i, table: (table[BOX, i + start], 4, 0))
    return [spec((PREV, OWN, NEXT)[k]) for k in sides] + [target]


def tile_scratch(leaf):
    return [pltpu.VMEM((64, leaf), bf16), pltpu.VMEM((leaf, 32), bf16), pltpu.VMEM((32, leaf), bf16)]


def near_early(start, units, table, packed, halo=None):
    _, rows, leaf = packed.shape
    sides = (1,) if halo is None else (0, 1, 2)
    arrays = (packed,) if halo is None else (halo[0], packed, halo[1])
    return pl.pallas_call(
        functools.partial(early_kernel, start, sides),
        grid_spec=pltpu.PrefetchScalarGridSpec(
            num_scalar_prefetch=1,
            grid=(units,),
            in_specs=source_specs(start, sides, rows, leaf),
            out_specs=pl.BlockSpec((1, 64, leaf), lambda i, table: (i, 0, 0)),
            scratch_shapes=tile_scratch(leaf),
        ),
        out_shape=jax.ShapeDtypeStruct((units, 64, leaf), f32),
        compiler_params=params(40),
        cost_estimate=SMALL,
        name="near_early",
    )(table, *arrays, packed)


def last_kernel(sides, table, *refs):
    sources = refs[: len(sides)]
    target_ref, potential_ref, transfer_ref, down_ref, *refs = refs[len(sides) :]
    *early, out_ref, held, left, right, total_ref = refs
    column = pl.program_id(0) + LAST_AT
    box = table[BOX, column]

    @pl.when(table[OPENS, column] == 1)
    def _():
        total_ref[...] = jnp.zeros_like(total_ref)
        at = 0
        for ref in early:
            for k in range(ref.shape[0]):

                @pl.when((table[LIVE, at] == 1) & (table[BOX, at] == box))
                def _(ref=ref, k=k):
                    total_ref[...] += ref[k]

                at += 1

    @pl.when(table[LIVE, column] == 1)
    def _():
        load_source(table, column, list(zip(sides, sources)), held, left)
        right[...] = target_features(target_ref[0].astype(f32))

        def write(cols, total):
            total_ref[:, cols] += total

        near_tile(held, left, right, write)

    @pl.when(table[CLOSES, column] == 1)
    def _():
        box_potential = dot_nt(potential_ref[...], transfer_ref[0]).astype(bf16)
        out_ref[0] = (dot(box_potential, down_ref[0]) + total_ref[...] * LN2).astype(bf16)


def near_last(table, packed, halo, potential, box_transfer, down_basis, early):
    boxes, rows, leaf = packed.shape
    rank = down_basis.shape[1]
    sides = (0, 1, 2)

    def whole(shape):
        return pl.BlockSpec(shape, lambda i, table: (0,) * len(shape))

    def by_box(shape):
        return pl.BlockSpec(shape, lambda i, table: (table[BOX, i + LAST_AT], 0, 0))

    return pl.pallas_call(
        functools.partial(last_kernel, sides),
        grid_spec=pltpu.PrefetchScalarGridSpec(
            num_scalar_prefetch=1,
            grid=(LAST_UNITS,),
            in_specs=source_specs(LAST_AT, sides, rows, leaf)
            + [whole((64, rank)), by_box((1, rank, rank)), by_box((1, rank, leaf))]
            + [pl.BlockSpec(part.shape, lambda i, table: (0, 0, 0), pipeline_mode=pl.Buffered(1)) for part in early],
            out_specs=by_box((1, 64, leaf)),
            scratch_shapes=tile_scratch(leaf) + [pltpu.VMEM((64, leaf), f32)],
        ),
        out_shape=jax.ShapeDtypeStruct((boxes, 64, leaf), bf16),
        compiler_params=params(40),
        cost_estimate=SMALL,
        name="near_last",
    )(table, halo[0], packed, halo[1], packed, potential, box_transfer, down_basis, *early)


def group_kernel(place_ref, skel_ref, nodes_ref, out_ref):
    nodes, _, rank = nodes_ref.shape
    total = jnp.zeros((64, rank), f32)
    found = jnp.zeros((16, rank), f32)
    skeleton = skel_ref[pl.ds(place_ref[0], 1), :]
    for k in range(nodes):
        total = total + nodes_ref[k, 80:144, :].astype(f32)
        found = found + dot(nodes_ref[k, 64:80, :], one_hot(skeleton, rank, k * rank))
    out_ref[...] = jnp.zeros_like(out_ref)
    out_ref[0:64, :] = total.astype(bf16)
    out_ref[64:80, :] = found.astype(bf16)


def group_pass(place, group_skeleton, nodes):
    rank = nodes.shape[2]
    return pl.pallas_call(
        group_kernel,
        in_specs=[SMEM] + [VMEM] * 2,
        out_specs=VMEM,
        out_shape=jax.ShapeDtypeStruct((GROUP_ROWS, rank), bf16),
        compiler_params=params(16),
        name="group_pass",
    )(place, group_skeleton, nodes)


def far_kernel(group_at_ref, node_at_ref, list_ref, nodes_ref, groups_ref, node_transfer_ref, out_ref):
    tx_index, ty_index = group_at_ref[0], node_at_ref[0]
    target = target_features(groups_ref[tx_index, 64:80, :].astype(f32))
    total = jnp.zeros(out_ref.shape, f32)
    for k in range(groups_ref.shape[0]):
        left = source_features(groups_ref[k, 64:80, :].astype(f32))
        term = dot(groups_ref[k, 0:64, :], entries(dot(left, target)))
        total = total + jnp.where(k != tx_index, term, 0.0)
    group_potential = (total * LN2).astype(bf16)
    target = target_features(nodes_ref[ty_index, 64:80, :].astype(f32))
    total = jnp.zeros(out_ref.shape, f32)
    for k in range(list_ref.shape[1]):
        slot = jnp.clip(list_ref[0, k] - tx_index * nodes_ref.shape[0], 0, nodes_ref.shape[0] - 1)
        left = source_features(nodes_ref[slot, 64:80, :].astype(f32))
        total = total + dot(nodes_ref[slot, 0:64, :], entries(dot(left, target)))
    out_ref[...] = (total * LN2 + dot_nt(group_potential, node_transfer_ref[0])).astype(bf16)


def far_pass(group_at, node_at, node_list, nodes, groups, node_transfer):
    rank = nodes.shape[2]
    return pl.pallas_call(
        far_kernel,
        in_specs=[SMEM] * 3 + [VMEM] * 3,
        out_specs=VMEM,
        out_shape=jax.ShapeDtypeStruct((64, rank), bf16),
        compiler_params=params(16),
        cost_estimate=SMALL,
        name="far_pass",
    )(group_at, node_at, node_list, nodes, groups, node_transfer)


def shards(
    probes,
    points,
    up_basis,
    down_basis,
    box_skeleton,
    box_transfer,
    node_skeleton,
    node_transfer,
    group_skeleton,
    near_list,
    node_list,
):
    boxes = probes.shape[0]
    n_tx = lax.axis_size("tx")
    n_ty = lax.axis_size("ty")
    tx_index = lax.axis_index("tx")
    ty_index = lax.axis_index("ty")
    node = tx_index * n_ty + ty_index
    base = ((node - 1) * boxes).astype(i32).reshape(1)

    group_at = tx_index.astype(i32).reshape(1)
    node_at = ty_index.astype(i32).reshape(1)
    packed, table, own = prep(
        near_list, base, probes, points, up_basis, box_skeleton, box_transfer, node_skeleton, node_transfer
    )
    prev_box = lax.ppermute(packed, "ty", [(i, i + 1) for i in range(n_ty - 1)])
    next_box = lax.ppermute(packed, "ty", [(i + 1, i) for i in range(n_ty - 1)])
    nodes = lax.all_gather(own, "ty", axis=0, tiled=False)
    halo = (prev_box, next_box)
    first = near_early(0, OWN_UNITS, table, packed)
    late_table, first = lax.optimization_barrier((table, first))
    second = near_early(OWN_UNITS, FIRST_LATE, late_table, packed, halo)
    second, nodes = lax.optimization_barrier((second, nodes))

    group = group_pass(group_at, group_skeleton, nodes)
    third_table, group = lax.optimization_barrier((late_table, group))
    groups = lax.all_gather(group, "tx", axis=0, tiled=False)
    third = near_early(OWN_UNITS + FIRST_LATE, LATE_UNITS - FIRST_LATE, third_table, packed, halo)
    third, groups = lax.optimization_barrier((third, groups))

    potential = far_pass(group_at, node_at, node_list, nodes, groups, node_transfer)
    return near_last(table, packed, halo, potential, box_transfer, down_basis, (first, second, third))


def solution(mesh):
    spec3 = P(("tx", "ty"), None, None)
    spec2 = P(("tx", "ty"), None)
    in_specs = (spec3, spec3, spec3, spec3, spec2, spec3, spec2, spec3, P(), spec2, spec2)
    return jax.shard_map(shards, mesh=mesh, in_specs=in_specs, out_specs=spec3, check_vma=False)
```

profile of v0, /device:TPU:28, one launch (start us, length us, event | category | flops | bytes accessed | tf_op | source)
XLA Modules:
  0.0 156.3 jit_solution(17797815028622695603)
XLA Ops:
  6.5 0.0 all-gather.5.cloned.1.call-start
  6.5 7.4 %prep.1 = (bf16[4,80,2048]{2,1,0:T(8,128)(2,1)}, s32[8,18]{1,0:T(8,128)}, bf16[144,256]{1,0:T(8,128)(2,1)}) custom-call(s32[4,3]{1,0:T(4,128)} %near_ref.1, s32[1]{0:T(128)} %bitcast.base_ref, bf16[4,64,2048]{2,1,0:T(8,128)(2,1)} %probes_ref.1, f32[4,8,2048]{2,1,0:T(8,128)} %points_ref.1, bf16[4,256,2048]{2,1,0:T(8,128)(2,1)} %up_ref.1, ...), custom_call_target="tpu_custom_call" | custom-call | tf_op jit(solution)/shard_map/prep/pallas_call | solution.py:209
  13.9 0.0 all-gather.5.cloned.1.call-update
  14.0 0.0 all-gather.7.cloned.1.call-start
  14.0 2.4 %collective-permute-start.1 = (bf16[4,80,2048]{2,1,0:T(8,128)(2,1)}, bf16[4,80,2048]{2,1,0:T(8,128)(2,1)S(1)}, u32[]{:S(2)}, u32[]{:S(2)}) collective-permute-start(bf16[4,80,2048]{2,1,0:T(8,128)(2,1)} %get-tuple-element.17.refs_0_.refs_1_.refs_3_), channel_id=1, source_target_pairs={{1,0},{2,1},{3,2},{4,3},{5,4},{6,5},{7,6},{8,7},{9,8},{10,9},{11,1... | collective-permute-start | bytes 3932168 | tf_op jit(solution)/shard_map/ppermute | solution.py:461
  16.5 3.4 %collective-permute-start = (bf16[4,80,2048]{2,1,0:T(8,128)(2,1)}, bf16[4,80,2048]{2,1,0:T(8,128)(2,1)S(1)}, u32[]{:S(2)}, u32[]{:S(2)}) collective-permute-start(bf16[4,80,2048]{2,1,0:T(8,128)(2,1)} %get-tuple-element.17.refs_0_.refs_1_.refs_3_), channel_id=1, source_target_pairs={{0,1},{1,2},{2,3},{3,4},{4,5},{5,6},{6,7},{7,8},{8,9},{9,10},{10,1... | collective-permute-start | bytes 3932168 | tf_op jit(solution)/shard_map/ppermute | solution.py:460
  19.9 0.0 copy-start
  19.9 1.3 copy-done
  21.2 0.0 copy-start.17
  21.2 0.7 copy-done.17
  21.9 7.9 %near_early.3.refs_7_ = f32[4,64,2048]{2,1,0:T(8,128)S(1)} custom-call(s32[8,18]{1,0:T(8,128)S(1)} %copy-done.17, bf16[4,80,2048]{2,1,0:T(8,128)(2,1)S(1)} %copy-done, bf16[4,80,2048]{2,1,0:T(8,128)(2,1)S(1)} %copy-done), custom_call_target="tpu_custom_call" | custom-call | flops 1024 | bytes 1024 | tf_op jit(solution)/shard_map/near_early/pallas_call | solution.py:297
  29.8 0.0 copy-start.7
  29.8 1.3 copy-done.7
  31.2 0.0 copy-start.19
  31.2 0.0 copy-start.18
  31.2 16.7 %collective-permute-done.1.refs_2_ = bf16[4,80,2048]{2,1,0:T(8,128)(2,1)S(1)} collective-permute-done((bf16[4,80,2048]{2,1,0:T(8,128)(2,1)}, bf16[4,80,2048]{2,1,0:T(8,128)(2,1)S(1)}, u32[]{:S(2)}, u32[]{:S(2)}) %collective-permute-start.1) | collective-permute-done | bytes 1310752 | tf_op jit(solution)/shard_map/ppermute | solution.py:461
  47.8 2.2 %collective-permute-done.refs_0_ = bf16[4,80,2048]{2,1,0:T(8,128)(2,1)S(1)} collective-permute-done((bf16[4,80,2048]{2,1,0:T(8,128)(2,1)}, bf16[4,80,2048]{2,1,0:T(8,128)(2,1)S(1)}, u32[]{:S(2)}, u32[]{:S(2)}) %collective-permute-start) | collective-permute-done | bytes 1310752 | tf_op jit(solution)/shard_map/ppermute | solution.py:460
  50.0 22.6 %near_early.4.refs_8_ = f32[3,64,2048]{2,1,0:T(8,128)S(1)} custom-call(s32[8,18]{1,0:T(8,128)S(1)} %copy-done.17, bf16[4,80,2048]{2,1,0:T(8,128)(2,1)S(1)} %collective-permute-done.refs_0_, bf16[4,80,2048]{2,1,0:T(8,128)(2,1)S(1)} %copy-done, bf16[4,80,2048]{2,1,0:T(8,128)(2,1)S(1)} %collective-permute-done.1.refs_2_, bf16[4,80,2048]{2,1,0:T(8,128)(2,1)S(1)} %copy-done), custom_call_target="tpu_custom_call" | custom-call | flops 1024 | bytes 1024 | tf_op jit(solution)/shard_map/near_early/pallas_call | solution.py:297
  72.6 0.0 copy-start.2
  72.6 1.1 copy-done.2
  73.7 0.0 copy-start.9
  73.7 1.2 copy-done.9
  74.8 0.0 copy-start.1
  74.8 0.0 all-gather.5.cloned.1.call-done
  74.8 0.0 copy-done.19
  74.8 0.0 copy-start.11
  74.9 1.4 copy-done.11
  76.2 1.0 group_pass.1
  77.3 0.0 all-gather.7.cloned.1.call-update
  77.3 0.0 copy-done.18
  77.3 0.0 copy-done.1
  77.3 0.0 copy-start.3
  77.3 1.3 copy-done.3
  78.6 0.0 copy-start.16
  78.6 0.0 copy-start.20
  78.6 0.0 copy-start.14
  78.6 29.9 %near_early.5.refs_9_ = f32[4,64,2048]{2,1,0:T(8,128)S(1)} custom-call(s32[8,18]{1,0:T(8,128)S(1)} %copy-done.18, bf16[4,80,2048]{2,1,0:T(8,128)(2,1)S(1)} %copy-done.3, bf16[4,80,2048]{2,1,0:T(8,128)(2,1)S(1)} %copy-done.1, bf16[4,80,2048]{2,1,0:T(8,128)(2,1)S(1)} %collective-permute-done.1.refs_2_, bf16[4,80,2048]{2,1,0:T(8,128)(2,1)S(1)} %copy-done.1), custom_call_target="tpu_custom_call" | custom-call | flops 1024 | bytes 1024 | tf_op jit(solution)/shard_map/near_early/pallas_call | solution.py:297
  108.5 0.0 copy-start.5
  108.5 1.3 copy-done.5
  109.8 0.0 all-gather.7.cloned.1.call-done
  109.8 0.0 copy-start.4
  109.8 0.0 copy-done.16
  109.8 0.0 copy-done.20
  109.8 0.0 copy-start.12
  109.9 1.4 copy-done.12
  111.2 0.0 copy-start.15
  111.2 1.2 copy-done.15
  112.5 3.4 %far_pass.1.refs_4_ = bf16[64,256]{1,0:T(8,128)(2,1)S(1)} custom-call(s32[1]{0:T(128)} %bitcast.1.place_ref.group_at_ref, s32[1]{0:T(128)} %bitcast.2.node_at_ref, s32[1,8]{1,0:T(1,128)S(1)} %copy-done.20, bf16[16,144,256]{2,1,0:T(8,128)(2,1)S(1)} %bitcast.6, bf16[8,256,256]{2,1,0:T(8,128)(2,1)S(1)} %bitcast.7, bf16[1,256,256]{2,1,0:T(8,128)(2,1)S(1)} %copy-done.16), custom_call_target="tpu_custom_call" | custom-call | flops 1024 | bytes 1024 | tf_op jit(solution)/shard_map/far_pass/pallas_call | solution.py:423
  115.9 0.0 copy-done.14
  115.9 0.0 copy-done.4
  115.9 0.0 copy-start.6
  115.9 1.6 %copy-done.6 = f32[4,64,2048]{2,1,0:T(8,128)S(1)} copy-done((f32[4,64,2048]{2,1,0:T(8,128)S(1)}, f32[4,64,2048]{2,1,0:T(8,128)}, u32[]{:S(2)}) %copy-start.6) | copy-done | bytes 2097176
  117.5 0.0 copy-start.8
  117.5 1.6 %copy-done.8 = f32[4,64,2048]{2,1,0:T(8,128)S(1)} copy-done((f32[4,64,2048]{2,1,0:T(8,128)S(1)}, f32[4,64,2048]{2,1,0:T(8,128)}, u32[]{:S(2)}) %copy-start.8) | copy-done | bytes 2097176
  119.1 0.0 copy-start.10
  119.1 1.4 copy-done.10
  120.5 0.0 copy-start.13
  120.5 2.2 %copy-done.13 = bf16[4,256,2048]{2,1,0:T(8,128)(2,1)S(1)} copy-done((bf16[4,256,2048]{2,1,0:T(8,128)(2,1)S(1)}, bf16[4,256,2048]{2,1,0:T(8,128)(2,1)}, u32[]{:S(2)}) %copy-start.13) | copy-done | bytes 4194328
  122.7 26.8 %near_last.1 = bf16[4,64,2048]{2,1,0:T(8,128)(2,1)} custom-call(s32[8,18]{1,0:T(8,128)S(1)} %copy-done.18, bf16[4,80,2048]{2,1,0:T(8,128)(2,1)S(1)} %copy-done.4, bf16[4,80,2048]{2,1,0:T(8,128)(2,1)S(1)} %copy-done.1, bf16[4,80,2048]{2,1,0:T(8,128)(2,1)S(1)} %collective-permute-done.1.refs_2_, bf16[4,80,2048]{2,1,0:T(8,128)(2,1)S(1)} %copy-done.1, ...), custom_call_target="tpu_custom_call" | custom-call | flops 1024 | bytes 1024 | tf_op jit(solution)/shard_map/near_last/pallas_call | solution.py:360
Async XLA Ops:
  6.5 68.3 %all-gather.5.cloned.1.call-start = ((), (), s32[]{:S(2)}) async-start(), calls=%async_computation | async-start | bytes 1253376 | tf_op jit(solution)/shard_map/all_gather | solution.py:462
  14.0 95.9 %all-gather.7.cloned.1.call-start = ((), (), s32[]{:S(2)}) async-start(), calls=%async_computation.1 | async-start | bytes 1179648 | tf_op jit(solution)/shard_map/all_gather | solution.py:471
  14.0 33.8 %collective-permute-start.1 = (bf16[4,80,2048]{2,1,0:T(8,128)(2,1)}, bf16[4,80,2048]{2,1,0:T(8,128)(2,1)S(1)}, u32[]{:S(2)}, u32[]{:S(2)}) collective-permute-start(bf16[4,80,2048]{2,1,0:T(8,128)(2,1)} %get-tuple-element.17.refs_0_.refs_1_.refs_3_), channel_id=1, source_target_pairs={{1,0},{2,1},{3,2},{4,3},{5,4},{6,5},{7,6},{8,7},{9,8},{10,9},{11,1... | collective-permute-start | bytes 3932168 | tf_op jit(solution)/shard_map/ppermute | solution.py:461
  16.5 33.5 %collective-permute-start = (bf16[4,80,2048]{2,1,0:T(8,128)(2,1)}, bf16[4,80,2048]{2,1,0:T(8,128)(2,1)S(1)}, u32[]{:S(2)}, u32[]{:S(2)}) collective-permute-start(bf16[4,80,2048]{2,1,0:T(8,128)(2,1)} %get-tuple-element.17.refs_0_.refs_1_.refs_3_), channel_id=1, source_target_pairs={{0,1},{1,2},{2,3},{3,4},{4,5},{5,6},{6,7},{7,8},{8,9},{9,10},{10,1... | collective-permute-start | bytes 3932168 | tf_op jit(solution)/shard_map/ppermute | solution.py:460
  19.9 1.3 copy-start
  21.2 0.7 copy-start.17
  29.8 1.3 copy-start.7
  31.2 43.7 %copy-start.19 = (s32[8,256]{1,0:T(8,128)S(1)}, s32[8,256]{1,0:T(8,128)}, u32[]{:S(2)}) copy-start(s32[8,256]{1,0:T(8,128)} %skel_ref.1) | copy-start | bytes 24580
  31.2 46.1 %copy-start.18 = (s32[8,18]{1,0:T(8,128)S(1)}, s32[8,18]{1,0:T(8,128)}, u32[]{:S(2)}) copy-start(s32[8,18]{1,0:T(8,128)} %get-tuple-element.21.table) | copy-start | bytes 1732
  72.6 1.1 copy-start.2
  73.7 1.2 copy-start.9
  74.8 2.5 %copy-start.1 = (bf16[4,80,2048]{2,1,0:T(8,128)(2,1)S(1)}, bf16[4,80,2048]{2,1,0:T(8,128)(2,1)}, u32[]{:S(2)}) copy-start(bf16[4,80,2048]{2,1,0:T(8,128)(2,1)} %get-tuple-element.17.refs_0_.refs_1_.refs_3_) | copy-start | bytes 3932164
  74.8 1.4 copy-start.11
  77.3 1.3 copy-start.3
  78.6 31.2 %copy-start.16 = (bf16[1,256,256]{2,1,0:T(8,128)(2,1)S(1)}, bf16[1,256,256]{2,1,0:T(8,128)(2,1)}, u32[]{:S(2)}) copy-start(bf16[1,256,256]{2,1,0:T(8,128)(2,1)} %node_transfer_ref.3) | copy-start | bytes 393220
  78.6 31.2 %copy-start.20 = (s32[1,8]{1,0:T(1,128)S(1)}, s32[1,8]{1,0:T(1,128)}, u32[]{:S(2)}) copy-start(s32[1,8]{1,0:T(1,128)} %list_ref.1) | copy-start | bytes 100
  78.6 37.2 %copy-start.14 = (bf16[4,256,256]{2,1,0:T(8,128)(2,1)S(1)}, bf16[4,256,256]{2,1,0:T(8,128)(2,1)}, u32[]{:S(2)}) copy-start(bf16[4,256,256]{2,1,0:T(8,128)(2,1)} %refs_5_.1) | copy-start | bytes 1572868
  108.5 1.3 copy-start.5
  109.8 6.0 %copy-start.4 = (bf16[4,80,2048]{2,1,0:T(8,128)(2,1)S(1)}, bf16[4,80,2048]{2,1,0:T(8,128)(2,1)}, u32[]{:S(2)}) copy-start(bf16[4,80,2048]{2,1,0:T(8,128)(2,1)} %copy-done.2) | copy-start | bytes 3932164
  109.8 1.4 copy-start.12
  111.2 1.2 copy-start.15
  115.9 1.6 %copy-start.6 = (f32[4,64,2048]{2,1,0:T(8,128)S(1)}, f32[4,64,2048]{2,1,0:T(8,128)}, u32[]{:S(2)}) copy-start(f32[4,64,2048]{2,1,0:T(8,128)} %copy-done.5) | copy-start | bytes 6291460
  117.5 1.6 %copy-start.8 = (f32[4,64,2048]{2,1,0:T(8,128)S(1)}, f32[4,64,2048]{2,1,0:T(8,128)}, u32[]{:S(2)}) copy-start(f32[4,64,2048]{2,1,0:T(8,128)} %copy-done.7) | copy-start | bytes 6291460
  119.1 1.4 copy-start.10
  120.5 2.2 %copy-start.13 = (bf16[4,256,2048]{2,1,0:T(8,128)(2,1)S(1)}, bf16[4,256,2048]{2,1,0:T(8,128)(2,1)}, u32[]{:S(2)}) copy-start(bf16[4,256,2048]{2,1,0:T(8,128)(2,1)} %refs_6_.1) | copy-start | bytes 12582916
Sparse Core Ops, SparseCore 0:
  14.1 56.4 all-gather.4
  77.4 27.0 all-gather.6
where the time goes:
time: 155 us; the launch traced here: 156 us
  Pallas kernels  99 us (64%)
  waiting for transfers between devices  18.9 us (12%)
  local copies, waits for them, and re-layouts  18.9 us (12%)
  between operations  13.6 us (9%)
  starting transfers between devices  5.88 us (4%)
    pallas_call x3, Pallas kernels, near_early(): pl.pallas_call(functools.partial(early_kernel, start, sides), grid_spec=p...  60.4 us
    pallas_call x1, Pallas kernels, near_last(): pl.pallas_call(functools.partial(last_kernel, sides), grid_spec=pltpu.Pre...  26.8 us
    unnamed x42, local copies, waits for them, and re-layouts  18.9 us
    ppermute x1, waiting for transfers between devices, shards(): next_box = lax.ppermute(packed, 'ty', [(i + 1, i) for i in range(n_ty - 1)])  16.7 us
    pallas_call x1, Pallas kernels, prep(): pl.pallas_call(prep_kernel, grid=(boxes,), in_specs=[SMEM, SMEM, by_box((...  7.39 us
    pallas_call x1, Pallas kernels, far_pass(): pl.pallas_call(far_kernel, in_specs=[SMEM] * 3 + [VMEM] * 3, out_specs=VM...  3.41 us
    ppermute x1, starting transfers between devices, shards(): prev_box = lax.ppermute(packed, 'ty', [(i, i + 1) for i in range(n_ty - 1)])  3.4 us
  transfers between devices with their start and end apart: 4, of which 2 were waited for; matrix products, arithmetic and copies ran while one was open for 0% of the time, Pallas kernels for 39%

commit v1 on v0

--- a/solution.py
+++ b/solution.py
@@ -17,14 +17,14 @@
 SCALE = INV_LENGTH / LN2
 VMEM = pl.BlockSpec(memory_space=pltpu.VMEM)
 SMEM = pl.BlockSpec(memory_space=pltpu.SMEM)
-TILE_ROWS = 1024
+TILE_ROWS = 512
 TILE_COLS = 256
 OWN_UNITS = 4
-LATE_UNITS = 7
+LATE_UNITS = 8
 FIRST_LATE = 3
 GROUP_ROWS = 256
 LAST_AT = OWN_UNITS + LATE_UNITS
-LAST_UNITS = 7
+LAST_UNITS = 6
 COLUMNS = LAST_AT + LAST_UNITS
 SIDE, BOX, LIVE, OPENS, CLOSES, PREV, OWN, NEXT = range(8)
 
@@ -304,7 +304,7 @@
             scratch_shapes=tile_scratch(leaf),
         ),
         out_shape=jax.ShapeDtypeStruct((units, 64, leaf), f32),
-        compiler_params=params(40),
+        compiler_params=params(),
         cost_estimate=SMALL,
         name="near_early",
     )(table, *arrays, packed)
@@ -369,7 +369,7 @@
             scratch_shapes=tile_scratch(leaf) + [pltpu.VMEM((64, leaf), f32)],
         ),
         out_shape=jax.ShapeDtypeStruct((boxes, 64, leaf), bf16),
-        compiler_params=params(40),
+        compiler_params=params(),
         cost_estimate=SMALL,
         name="near_last",
     )(table, halo[0], packed, halo[1], packed, potential, box_transfer, down_basis, *early)
@@ -395,7 +395,7 @@
         in_specs=[SMEM] + [VMEM] * 2,
         out_specs=VMEM,
         out_shape=jax.ShapeDtypeStruct((GROUP_ROWS, rank), bf16),
-        compiler_params=params(16),
+        compiler_params=params(),
         name="group_pass",
     )(place, group_skeleton, nodes)
 
@@ -425,7 +425,7 @@
         in_specs=[SMEM] * 3 + [VMEM] * 3,
         out_specs=VMEM,
         out_shape=jax.ShapeDtypeStruct((64, rank), bf16),
-        compiler_params=params(16),
+        compiler_params=params(),
         cost_estimate=SMALL,
         name="far_pass",
     )(group_at, node_at, node_list, nodes, groups, node_transfer)

time: 155 us -> 135 us (0.87)
  the two profiles are of different devices: /device:TPU:28 before, /device:TPU:45 now
where the time goes in v1:
time: 135 us; the launch traced here: 134 us
  Pallas kernels  88.6 us (66%)
  waiting for transfers between devices  26.3 us (19%)
  between operations  13.4 us (10%)
  starting transfers between devices  5.33 us (4%)
    pallas_call x3, Pallas kernels, near_early(): pl.pallas_call(functools.partial(early_kernel, start, sides), grid_spec=p...  53.3 us
    ppermute x1, waiting for transfers between devices, shards(): next_box = lax.ppermute(packed, 'ty', [(i + 1, i) for i in range(n_ty - 1)])  24.2 us
    pallas_call x1, Pallas kernels, near_last(): pl.pallas_call(functools.partial(last_kernel, sides), grid_spec=pltpu.Pre...  20.5 us
    pallas_call x1, Pallas kernels, prep(): pl.pallas_call(prep_kernel, grid=(boxes,), in_specs=[SMEM, SMEM, by_box((...  7.39 us
    pallas_call x1, Pallas kernels, far_pass(): pl.pallas_call(far_kernel, in_specs=[SMEM] * 3 + [VMEM] * 3, out_specs=VM...  5.08 us
    ppermute x1, starting transfers between devices, shards(): prev_box = lax.ppermute(packed, 'ty', [(i, i + 1) for i in range(n_ty - 1)])  3.12 us
  transfers between devices with their start and end apart: 4, of which 3 were waited for; matrix products, arithmetic and copies ran while one was open for 0% of the time, Pallas kernels for 40%

profile of v1, /device:TPU:45, one launch (start us, length us, event | category | flops | bytes accessed | tf_op | source)
XLA Modules:
  0.0 133.6 jit_solution(16014370422965419416)
XLA Ops:
  6.5 0.0 all-gather.5.cloned.1.call-start
  6.5 7.4 %prep.1 = (bf16[4,80,2048]{2,1,0:T(8,128)(2,1)}, s32[8,18]{1,0:T(8,128)}, bf16[144,256]{1,0:T(8,128)(2,1)}) custom-call(s32[4,3]{1,0:T(4,128)} %near_ref.1, s32[1]{0:T(128)} %bitcast.base_ref, bf16[4,64,2048]{2,1,0:T(8,128)(2,1)} %probes_ref.1, f32[4,8,2048]{2,1,0:T(8,128)} %points_ref.1, bf16[4,256,2048]{2,1,0:T(8,128)(2,1)} %up_ref.1, ...), custom_call_target="tpu_custom_call" | custom-call | tf_op jit(solution)/shard_map/prep/pallas_call | solution.py:209
  13.9 0.0 all-gather.5.cloned.1.call-update
  14.0 0.0 all-gather.7.cloned.1.call-start
  14.0 2.2 %collective-permute-start.1 = (bf16[4,80,2048]{2,1,0:T(8,128)(2,1)}, bf16[4,80,2048]{2,1,0:T(8,128)(2,1)S(1)}, u32[]{:S(2)}, u32[]{:S(2)}) collective-permute-start(bf16[4,80,2048]{2,1,0:T(8,128)(2,1)} %get-tuple-element.17.refs_0_.refs_1_.refs_3_), channel_id=1, source_target_pairs={{1,0},{2,1},{3,2},{4,3},{5,4},{6,5},{7,6},{8,7},{9,8},{10,9},{11,1... | collective-permute-start | bytes 3932168 | tf_op jit(solution)/shard_map/ppermute | solution.py:461
  16.2 3.1 %collective-permute-start = (bf16[4,80,2048]{2,1,0:T(8,128)(2,1)}, bf16[4,80,2048]{2,1,0:T(8,128)(2,1)}, u32[]{:S(2)}, u32[]{:S(2)}) collective-permute-start(bf16[4,80,2048]{2,1,0:T(8,128)(2,1)} %get-tuple-element.17.refs_0_.refs_1_.refs_3_), channel_id=1, source_target_pairs={{0,1},{1,2},{2,3},{3,4},{4,5},{5,6},{6,7},{7,8},{8,9},{9,10},{10,1... | collective-permute-start | bytes 3932168 | tf_op jit(solution)/shard_map/ppermute | solution.py:460
  19.3 3.5 %near_early.3.refs_7_ = f32[4,64,2048]{2,1,0:T(8,128)} custom-call(s32[8,18]{1,0:T(8,128)} %get-tuple-element.21.table, bf16[4,80,2048]{2,1,0:T(8,128)(2,1)} %get-tuple-element.17.refs_0_.refs_1_.refs_3_, bf16[4,80,2048]{2,1,0:T(8,128)(2,1)} %get-tuple-element.17.refs_0_.refs_1_.refs_3_), custom_call_target="tpu_custom_call" | custom-call | flops 1024 | bytes 1024 | tf_op jit(solution)/shard_map/near_early/pallas_call | solution.py:297
  22.8 24.2 %collective-permute-done.1.refs_2_ = bf16[4,80,2048]{2,1,0:T(8,128)(2,1)S(1)} collective-permute-done((bf16[4,80,2048]{2,1,0:T(8,128)(2,1)}, bf16[4,80,2048]{2,1,0:T(8,128)(2,1)S(1)}, u32[]{:S(2)}, u32[]{:S(2)}) %collective-permute-start.1) | collective-permute-done | bytes 1310752 | tf_op jit(solution)/shard_map/ppermute | solution.py:461
  47.1 0.0 copy-start
  47.1 1.8 %collective-permute-done.refs_0_ = bf16[4,80,2048]{2,1,0:T(8,128)(2,1)} collective-permute-done((bf16[4,80,2048]{2,1,0:T(8,128)(2,1)}, bf16[4,80,2048]{2,1,0:T(8,128)(2,1)}, u32[]{:S(2)}, u32[]{:S(2)}) %collective-permute-start) | collective-permute-done | bytes 1310752 | tf_op jit(solution)/shard_map/ppermute | solution.py:460
  48.9 0.0 copy-done
  48.9 19.3 %near_early.4.refs_8_ = f32[3,64,2048]{2,1,0:T(8,128)} custom-call(s32[8,18]{1,0:T(8,128)} %get-tuple-element.21.table, bf16[4,80,2048]{2,1,0:T(8,128)(2,1)} %collective-permute-done.refs_0_, bf16[4,80,2048]{2,1,0:T(8,128)(2,1)} %get-tuple-element.17.refs_0_.refs_1_.refs_3_, bf16[4,80,2048]{2,1,0:T(8,128)(2,1)} %copy-done, ...), custom_call_target="tpu_custom_call" | custom-call | flops 1024 | bytes 1024 | tf_op jit(solution)/shard_map/near_early/pallas_call | solution.py:297
  68.2 0.2 all-gather.5.cloned.1.call-done
  68.3 2.3 %group_pass.1 = bf16[256,256]{1,0:T(8,128)(2,1)} custom-call(s32[1]{0:T(128)} %bitcast.1.place_ref.group_at_ref, s32[8,256]{1,0:T(8,128)} %skel_ref.1, bf16[16,144,256]{2,1,0:T(8,128)(2,1)} %bitcast.5), custom_call_target="tpu_custom_call" | custom-call | tf_op jit(solution)/shard_map/group_pass/pallas_call | solution.py:393
  70.7 0.0 all-gather.7.cloned.1.call-update
  70.7 30.6 %near_early.5.refs_9_ = f32[5,64,2048]{2,1,0:T(8,128)} custom-call(s32[8,18]{1,0:T(8,128)} %get-tuple-element.21.table, bf16[4,80,2048]{2,1,0:T(8,128)(2,1)} %collective-permute-done.refs_0_, bf16[4,80,2048]{2,1,0:T(8,128)(2,1)} %get-tuple-element.17.refs_0_.refs_1_.refs_3_, bf16[4,80,2048]{2,1,0:T(8,128)(2,1)} %copy-done, ...), custom_call_target="tpu_custom_call" | custom-call | flops 1024 | bytes 1024 | tf_op jit(solution)/shard_map/near_early/pallas_call | solution.py:297
  101.2 0.0 all-gather.7.cloned.1.call-done
  101.2 5.1 %far_pass.1.refs_4_ = bf16[64,256]{1,0:T(8,128)(2,1)} custom-call(s32[1]{0:T(128)} %bitcast.1.place_ref.group_at_ref, s32[1]{0:T(128)} %bitcast.2.node_at_ref, s32[1,8]{1,0:T(1,128)} %list_ref.1, bf16[16,144,256]{2,1,0:T(8,128)(2,1)} %bitcast.6, bf16[8,256,256]{2,1,0:T(8,128)(2,1)} %bitcast.7, bf16[1,256,256]{2,1,0:T(8,128)(2,1)} %node_transfer_ref.3), custom_call_target="tpu_custom_call" | custom-call | flops 1024 | bytes 1024 | tf_op jit(solution)/shard_map/far_pass/pallas_call | solution.py:423
  106.3 20.5 %near_last.1 = bf16[4,64,2048]{2,1,0:T(8,128)(2,1)} custom-call(s32[8,18]{1,0:T(8,128)} %get-tuple-element.21.table, bf16[4,80,2048]{2,1,0:T(8,128)(2,1)} %collective-permute-done.refs_0_, bf16[4,80,2048]{2,1,0:T(8,128)(2,1)} %get-tuple-element.17.refs_0_.refs_1_.refs_3_, bf16[4,80,2048]{2,1,0:T(8,128)(2,1)} %copy-done, ...), custom_call_target="tpu_custom_call" | custom-call | flops 1024 | bytes 1024 | tf_op jit(solution)/shard_map/near_last/pallas_call | solution.py:360
Async XLA Ops:
  6.5 61.8 %all-gather.5.cloned.1.call-start = ((), (), s32[]{:S(2)}) async-start(), calls=%async_computation | async-start | bytes 1253376 | tf_op jit(solution)/shard_map/all_gather | solution.py:462
  14.0 87.3 %all-gather.7.cloned.1.call-start = ((), (), s32[]{:S(2)}) async-start(), calls=%async_computation.1 | async-start | bytes 1179648 | tf_op jit(solution)/shard_map/all_gather | solution.py:471
  14.0 33.0 %collective-permute-start.1 = (bf16[4,80,2048]{2,1,0:T(8,128)(2,1)}, bf16[4,80,2048]{2,1,0:T(8,128)(2,1)S(1)}, u32[]{:S(2)}, u32[]{:S(2)}) collective-permute-start(bf16[4,80,2048]{2,1,0:T(8,128)(2,1)} %get-tuple-element.17.refs_0_.refs_1_.refs_3_), channel_id=1, source_target_pairs={{1,0},{2,1},{3,2},{4,3},{5,4},{6,5},{7,6},{8,7},{9,8},{10,9},{11,1... | collective-permute-start | bytes 3932168 | tf_op jit(solution)/shard_map/ppermute | solution.py:461
  16.2 32.7 %collective-permute-start = (bf16[4,80,2048]{2,1,0:T(8,128)(2,1)}, bf16[4,80,2048]{2,1,0:T(8,128)(2,1)}, u32[]{:S(2)}, u32[]{:S(2)}) collective-permute-start(bf16[4,80,2048]{2,1,0:T(8,128)(2,1)} %get-tuple-element.17.refs_0_.refs_1_.refs_3_), channel_id=1, source_target_pairs={{0,1},{1,2},{2,3},{3,4},{4,5},{5,6},{6,7},{7,8},{8,9},{9,10},{10,1... | collective-permute-start | bytes 3932168 | tf_op jit(solution)/shard_map/ppermute | solution.py:460
  47.1 1.8 %copy-start = (bf16[4,80,2048]{2,1,0:T(8,128)(2,1)}, bf16[4,80,2048]{2,1,0:T(8,128)(2,1)S(1)}, u32[]{:S(2)}) copy-start(bf16[4,80,2048]{2,1,0:T(8,128)(2,1)S(1)} %collective-permute-done.1.refs_2_) | copy-start | bytes 3932164
Sparse Core Ops, SparseCore 0:
  14.1 54.1 all-gather.4
  70.8 26.7 all-gather.6

commit v2 on v1

--- a/solution.py
+++ b/solution.py
@@ -20,11 +20,10 @@
 TILE_ROWS = 512
 TILE_COLS = 256
 OWN_UNITS = 4
-LATE_UNITS = 8
-FIRST_LATE = 3
+LATE_UNITS = 4
 GROUP_ROWS = 256
 LAST_AT = OWN_UNITS + LATE_UNITS
-LAST_UNITS = 6
+LAST_UNITS = 9
 COLUMNS = LAST_AT + LAST_UNITS
 SIDE, BOX, LIVE, OPENS, CLOSES, PREV, OWN, NEXT = range(8)
 
@@ -34,6 +33,7 @@
 
 
 SMALL = pl.CostEstimate(flops=1024, bytes_accessed=1024, transcendentals=0)
+LARGE = pl.CostEstimate(flops=2**40, bytes_accessed=2**28, transcendentals=0)
 
 
 def split_points(points):
@@ -161,7 +161,7 @@
     transfer_ref,
     node_skel_ref,
     node_transfer_ref,
-    packed_ref,
+    pair_ref,
     table_ref,
     out_ref,
     acc,
@@ -177,10 +177,9 @@
         write_table(near_ref, base_ref, table_ref)
         acc[...] = jnp.zeros_like(acc)
 
-    packed_ref[0, :64, :] = probes_ref[0]
     high, low = split_points(points_ref[0])
     pair = jnp.concatenate([high.astype(f32), low.astype(f32)], axis=0).astype(bf16)
-    packed_ref[0, 64:80, :] = pair
+    pair_ref[0] = pair
     weights = dot_nt(probes_ref[0], up_ref[0]).astype(bf16)
     acc[...] += dot(weights, transfer_ref[0])
     pool[b] = dot(pair, one_hot(box_skel_ref[pl.ds(b, 1), :], leaf)).astype(bf16)
@@ -220,9 +219,9 @@
             whole((1, rank)),
             whole((1, rank, rank)),
         ],
-        out_specs=[by_box((count + 16, leaf)), SMEM, whole((144, rank))],
+        out_specs=[by_box((16, leaf)), SMEM, whole((144, rank))],
         out_shape=[
-            jax.ShapeDtypeStruct((boxes, count + 16, leaf), bf16),
+            jax.ShapeDtypeStruct((boxes, 16, leaf), bf16),
             jax.ShapeDtypeStruct((8, COLUMNS), i32),
             jax.ShapeDtypeStruct((144, rank), bf16),
         ],
@@ -234,12 +233,12 @@
 
 def load_source(table, column, sources, held, left):
     side = table[SIDE, column]
-    for k, ref in sources:
+    for k, probes_ref, pair_ref in sources:
 
         @pl.when(side == k)
-        def _(ref=ref):
-            held[...] = ref[0, :64, :]
-            left[...] = source_features(ref[0, 64:80, :].astype(f32))
+        def _(probes_ref=probes_ref, pair_ref=pair_ref):
+            held[...] = probes_ref[0]
+            left[...] = source_features(pair_ref[0].astype(f32))
 
 
 def near_tile(held, left, right, write):
@@ -263,13 +262,14 @@
 
 
 def early_kernel(start, sides, table, *refs):
-    sources = refs[: len(sides)]
-    target_ref, out_ref, held, left, right = refs[len(sides) :]
+    count = len(sides)
+    sources = list(zip(sides, refs[:count], refs[count : 2 * count]))
+    target_ref, out_ref, held, left, right = refs[2 * count :]
     column = pl.program_id(0) + start
 
     @pl.when(table[LIVE, column] == 1)
     def _():
-        load_source(table, column, list(zip(sides, sources)), held, left)
+        load_source(table, column, sources, held, left)
         right[...] = target_features(target_ref[0].astype(f32))
 
         def write(cols, total):
@@ -278,101 +278,85 @@
         near_tile(held, left, right, write)
 
 
-def source_specs(start, sides, rows, leaf):
-    def spec(row):
+def source_specs(start, sides, leaf):
+    def spec(row, rows):
         return pl.BlockSpec((1, rows, leaf), lambda i, table: (table[row, i + start], 0, 0))
 
-    target = pl.BlockSpec((1, 16, leaf), lambda i, table: (table[BOX, i + start], 4, 0))
-    return [spec((PREV, OWN, NEXT)[k]) for k in sides] + [target]
+    named = [(PREV, OWN, NEXT)[k] for k in sides]
+    return [spec(row, 64) for row in named] + [spec(row, 16) for row in named] + [spec(BOX, 16)]
 
 
 def tile_scratch(leaf):
     return [pltpu.VMEM((64, leaf), bf16), pltpu.VMEM((leaf, 32), bf16), pltpu.VMEM((32, leaf), bf16)]
 
 
-def near_early(start, units, table, packed, halo=None):
-    _, rows, leaf = packed.shape
-    sides = (1,) if halo is None else (0, 1, 2)
-    arrays = (packed,) if halo is None else (halo[0], packed, halo[1])
+def near_early(start, units, table, sides, probes, pairs, own_pair, cost):
+    leaf = own_pair.shape[2]
     return pl.pallas_call(
         functools.partial(early_kernel, start, sides),
         grid_spec=pltpu.PrefetchScalarGridSpec(
             num_scalar_prefetch=1,
             grid=(units,),
-            in_specs=source_specs(start, sides, rows, leaf),
+            in_specs=source_specs(start, sides, leaf),
             out_specs=pl.BlockSpec((1, 64, leaf), lambda i, table: (i, 0, 0)),
             scratch_shapes=tile_scratch(leaf),
         ),
         out_shape=jax.ShapeDtypeStruct((units, 64, leaf), f32),
         compiler_params=params(),
-        cost_estimate=SMALL,
+        cost_estimate=cost,
         name="near_early",
-    )(table, *arrays, packed)
+    )(table, *probes, *pairs, own_pair)
 
 
 def last_kernel(sides, table, *refs):
-    sources = refs[: len(sides)]
-    target_ref, potential_ref, transfer_ref, down_ref, *refs = refs[len(sides) :]
-    *early, out_ref, held, left, right, total_ref = refs
+    count = len(sides)
+    sources = list(zip(sides, refs[:count], refs[count : 2 * count]))
+    target_ref, *early, out_ref, held, left, right = refs[2 * count :]
     column = pl.program_id(0) + LAST_AT
     box = table[BOX, column]
 
     @pl.when(table[OPENS, column] == 1)
     def _():
-        total_ref[...] = jnp.zeros_like(total_ref)
+        out_ref[...] = jnp.zeros_like(out_ref)
         at = 0
         for ref in early:
             for k in range(ref.shape[0]):
 
                 @pl.when((table[LIVE, at] == 1) & (table[BOX, at] == box))
                 def _(ref=ref, k=k):
-                    total_ref[...] += ref[k]
+                    out_ref[0] += ref[k]
 
                 at += 1
 
     @pl.when(table[LIVE, column] == 1)
     def _():
-        load_source(table, column, list(zip(sides, sources)), held, left)
+        load_source(table, column, sources, held, left)
         right[...] = target_features(target_ref[0].astype(f32))
 
         def write(cols, total):
-            total_ref[:, cols] += total
+            out_ref[0, :, cols] += total
 
         near_tile(held, left, right, write)
 
-    @pl.when(table[CLOSES, column] == 1)
-    def _():
-        box_potential = dot_nt(potential_ref[...], transfer_ref[0]).astype(bf16)
-        out_ref[0] = (dot(box_potential, down_ref[0]) + total_ref[...] * LN2).astype(bf16)
-
-
-def near_last(table, packed, halo, potential, box_transfer, down_basis, early):
-    boxes, rows, leaf = packed.shape
-    rank = down_basis.shape[1]
+
+def near_last(table, probes, pairs, own_pair, early):
+    boxes, _, leaf = own_pair.shape
     sides = (0, 1, 2)
-
-    def whole(shape):
-        return pl.BlockSpec(shape, lambda i, table: (0,) * len(shape))
-
-    def by_box(shape):
-        return pl.BlockSpec(shape, lambda i, table: (table[BOX, i + LAST_AT], 0, 0))
-
     return pl.pallas_call(
         functools.partial(last_kernel, sides),
         grid_spec=pltpu.PrefetchScalarGridSpec(
             num_scalar_prefetch=1,
             grid=(LAST_UNITS,),
-            in_specs=source_specs(LAST_AT, sides, rows, leaf)
-            + [whole((64, rank)), by_box((1, rank, rank)), by_box((1, rank, leaf))]
+            in_specs=source_specs(LAST_AT, sides, leaf)
             + [pl.BlockSpec(part.shape, lambda i, table: (0, 0, 0), pipeline_mode=pl.Buffered(1)) for part in early],
-            out_specs=by_box((1, 64, leaf)),
-            scratch_shapes=tile_scratch(leaf) + [pltpu.VMEM((64, leaf), f32)],
+            out_specs=pl.BlockSpec((1, 64, leaf), lambda i, table: (table[BOX, i + LAST_AT], 0, 0)),
+            scratch_shapes=tile_scratch(leaf),
         ),
-        out_shape=jax.ShapeDtypeStruct((boxes, 64, leaf), bf16),
+        out_shape=jax.ShapeDtypeStruct((boxes, 64, leaf), f32),
         compiler_params=params(),
         cost_estimate=SMALL,
         name="near_last",
-    )(table, halo[0], packed, halo[1], packed, potential, box_transfer, down_basis, *early)
+    )(table, *probes, *pairs, own_pair, *early)
 
 
 def group_kernel(place_ref, skel_ref, nodes_ref, out_ref):
@@ -400,35 +384,76 @@
     )(place, group_skeleton, nodes)
 
 
-def far_kernel(group_at_ref, node_at_ref, list_ref, nodes_ref, groups_ref, node_transfer_ref, out_ref):
-    tx_index, ty_index = group_at_ref[0], node_at_ref[0]
+def far_potential(tx_index, ty_index, list_ref, nodes_ref, groups_ref, node_transfer):
+    rank = nodes_ref.shape[2]
     target = target_features(groups_ref[tx_index, 64:80, :].astype(f32))
-    total = jnp.zeros(out_ref.shape, f32)
+    total = jnp.zeros((64, rank), f32)
     for k in range(groups_ref.shape[0]):
         left = source_features(groups_ref[k, 64:80, :].astype(f32))
         term = dot(groups_ref[k, 0:64, :], entries(dot(left, target)))
         total = total + jnp.where(k != tx_index, term, 0.0)
     group_potential = (total * LN2).astype(bf16)
     target = target_features(nodes_ref[ty_index, 64:80, :].astype(f32))
-    total = jnp.zeros(out_ref.shape, f32)
+    total = jnp.zeros((64, rank), f32)
     for k in range(list_ref.shape[1]):
         slot = jnp.clip(list_ref[0, k] - tx_index * nodes_ref.shape[0], 0, nodes_ref.shape[0] - 1)
         left = source_features(nodes_ref[slot, 64:80, :].astype(f32))
         total = total + dot(nodes_ref[slot, 0:64, :], entries(dot(left, target)))
-    out_ref[...] = (total * LN2 + dot_nt(group_potential, node_transfer_ref[0])).astype(bf16)
-
-
-def far_pass(group_at, node_at, node_list, nodes, groups, node_transfer):
-    rank = nodes.shape[2]
+    return (total * LN2 + dot_nt(group_potential, node_transfer)).astype(bf16)
+
+
+def down_kernel(
+    group_at_ref,
+    node_at_ref,
+    list_ref,
+    nodes_ref,
+    groups_ref,
+    node_transfer_ref,
+    transfer_ref,
+    down_ref,
+    near_ref,
+    out_ref,
+    potential,
+):
+    @pl.when(pl.program_id(0) == 0)
+    def _():
+        potential[...] = far_potential(
+            group_at_ref[0], node_at_ref[0], list_ref, nodes_ref, groups_ref, node_transfer_ref[0]
+        )
+
+    box_potential = dot_nt(potential[...], transfer_ref[0]).astype(bf16)
+    out_ref[0] = (dot(box_potential, down_ref[0]) + near_ref[0] * LN2).astype(bf16)
+
+
+def down_pass(group_at, node_at, node_list, nodes, groups, node_transfer, box_transfer, down_basis, near):
+    boxes, rank, leaf = down_basis.shape
+
+    def whole(shape):
+        return pl.BlockSpec(shape, lambda b: (0,) * len(shape))
+
+    def by_box(shape):
+        return pl.BlockSpec((1,) + shape, lambda b: (b, 0, 0))
+
     return pl.pallas_call(
-        far_kernel,
-        in_specs=[SMEM] * 3 + [VMEM] * 3,
-        out_specs=VMEM,
-        out_shape=jax.ShapeDtypeStruct((64, rank), bf16),
+        down_kernel,
+        grid=(boxes,),
+        in_specs=[
+            SMEM,
+            SMEM,
+            SMEM,
+            whole((nodes.shape[0], 80, rank)),
+            whole((groups.shape[0], 80, rank)),
+            whole((1, rank, rank)),
+            by_box((rank, rank)),
+            by_box((rank, leaf)),
+            by_box((64, leaf)),
+        ],
+        out_specs=by_box((64, leaf)),
+        out_shape=jax.ShapeDtypeStruct((boxes, 64, leaf), bf16),
+        scratch_shapes=[pltpu.VMEM((64, rank), bf16)],
         compiler_params=params(),
-        cost_estimate=SMALL,
-        name="far_pass",
-    )(group_at, node_at, node_list, nodes, groups, node_transfer)
+        name="down_pass",
+    )(group_at, node_at, node_list, nodes, groups, node_transfer, box_transfer, down_basis, near)
 
 
 def shards(
@@ -454,26 +479,26 @@
 
     group_at = tx_index.astype(i32).reshape(1)
     node_at = ty_index.astype(i32).reshape(1)
-    packed, table, own = prep(
+    forward = [(i, i + 1) for i in range(n_ty - 1)]
+    backward = [(i + 1, i) for i in range(n_ty - 1)]
+    sides = (0, 1, 2)
+    all_probes = (lax.ppermute(probes, "ty", forward), probes, lax.ppermute(probes, "ty", backward))
+    pair, table, own = prep(
         near_list, base, probes, points, up_basis, box_skeleton, box_transfer, node_skeleton, node_transfer
     )
-    prev_box = lax.ppermute(packed, "ty", [(i, i + 1) for i in range(n_ty - 1)])
-    next_box = lax.ppermute(packed, "ty", [(i + 1, i) for i in range(n_ty - 1)])
+    all_pairs = (lax.ppermute(pair, "ty", forward), pair, lax.ppermute(pair, "ty", backward))
     nodes = lax.all_gather(own, "ty", axis=0, tiled=False)
-    halo = (prev_box, next_box)
-    first = near_early(0, OWN_UNITS, table, packed)
+    first = near_early(0, OWN_UNITS, table, (1,), (probes,), (pair,), pair, SMALL)
     late_table, first = lax.optimization_barrier((table, first))
-    second = near_early(OWN_UNITS, FIRST_LATE, late_table, packed, halo)
+    second = near_early(OWN_UNITS, LATE_UNITS, late_table, sides, all_probes, all_pairs, pair, LARGE)
     second, nodes = lax.optimization_barrier((second, nodes))
 
     group = group_pass(group_at, group_skeleton, nodes)
     third_table, group = lax.optimization_barrier((late_table, group))
     groups = lax.all_gather(group, "tx", axis=0, tiled=False)
-    third = near_early(OWN_UNITS + FIRST_LATE, LATE_UNITS - FIRST_LATE, third_table, packed, halo)
-    third, groups = lax.optimization_barrier((third, groups))
-
-    potential = far_pass(group_at, node_at, node_list, nodes, groups, node_transfer)
-    return near_last(table, packed, halo, potential, box_transfer, down_basis, (first, second, third))
+    near = near_last(third_table, all_probes, all_pairs, pair, (first, second))
+    near, groups = lax.optimization_barrier((near, groups))
+    return down_pass(group_at, node_at, node_list, nodes, groups, node_transfer, box_transfer, down_basis, near)
 
 
 def solution(mesh):

time: 135 us -> 130 us (0.963)
  the two profiles are of different devices: /device:TPU:45 before, /device:TPU:66 now
where the time goes in v2:
time: 130 us
  Pallas kernels  91.9 us (71%)
  between operations  13.5 us (10%)
  starting transfers between devices  11.7 us (9%)
  waiting for transfers between devices  11.7 us (9%)
    pallas_call x1, Pallas kernels, near_last(): pl.pallas_call(functools.partial(last_kernel, sides), grid_spec=pltpu.Pre...  39.8 us
    pallas_call x2, Pallas kernels, near_early(): pl.pallas_call(functools.partial(early_kernel, start, sides), grid_spec=p...  34 us
    pallas_call x1, Pallas kernels, down_pass(): pl.pallas_call(down_kernel, grid=(boxes,), in_specs=[SMEM, SMEM, SMEM, wh...  8.56 us
    pallas_call x1, Pallas kernels, prep(): pl.pallas_call(prep_kernel, grid=(boxes,), in_specs=[SMEM, SMEM, by_box((...  7.19 us
    ppermute x1, waiting for transfers between devices, shards(): lax.ppermute(pair, 'ty', backward)  4.62 us
    all_gather x1, waiting for transfers between devices, shards(): nodes = lax.all_gather(own, 'ty', axis=0, tiled=False)  4.3 us
    ppermute x1, starting transfers between devices, shards(): lax.ppermute(probes, 'ty', forward)  3.4 us
    ppermute x1, starting transfers between devices, shards(): lax.ppermute(pair, 'ty', forward)  3.11 us
  transfers between devices with their start and end apart: 6, of which 3 were waited for; matrix products, arithmetic and copies ran while one was open for 0% of the time, Pallas kernels for 62%

profile of v2, /device:TPU:66, one launch (start us, length us, event | category | flops | bytes accessed | tf_op | source)
XLA Modules:
  0.0 129.9 jit_solution(5171798542923571653)
XLA Ops:
  6.5 0.0 all-gather.5.cloned.1.call-start
  6.5 2.4 %collective-permute-start.1 = (bf16[4,64,2048]{2,1,0:T(8,128)(2,1)}, bf16[4,64,2048]{2,1,0:T(8,128)(2,1)S(1)}, u32[]{:S(2)}, u32[]{:S(2)}) collective-permute-start(bf16[4,64,2048]{2,1,0:T(8,128)(2,1)} %refs_1_.3), channel_id=1, source_target_pairs={{1,0},{2,1},{3,2},{4,3},{5,4},{6,5},{7,6},{8,7},{9,8},{10,9},{11,1... | collective-permute-start | bytes 3145736 | tf_op jit(solution)/shard_map/ppermute | solution.py:485
  9.0 3.4 %collective-permute-start = (bf16[4,64,2048]{2,1,0:T(8,128)(2,1)}, bf16[4,64,2048]{2,1,0:T(8,128)(2,1)}, u32[]{:S(2)}, u32[]{:S(2)}) collective-permute-start(bf16[4,64,2048]{2,1,0:T(8,128)(2,1)} %refs_1_.3), channel_id=1, source_target_pairs={{0,1},{1,2},{2,3},{3,4},{4,5},{5,6},{6,7},{7,8},{8,9},{9,10},{10,1... | collective-permute-start | bytes 3145736 | tf_op jit(solution)/shard_map/ppermute | solution.py:485
  12.4 7.2 %prep.1 = (bf16[4,16,2048]{2,1,0:T(8,128)(2,1)}, s32[8,17]{1,0:T(8,128)}, bf16[144,256]{1,0:T(8,128)(2,1)}) custom-call(s32[4,3]{1,0:T(4,128)} %near_ref.1, s32[1]{0:T(128)} %bitcast.2.base_ref, bf16[4,64,2048]{2,1,0:T(8,128)(2,1)} %refs_1_.3, f32[4,8,2048]{2,1,0:T(8,128)} %points_ref.1, bf16[4,256,2048]{2,1,0:T(8,128)(2,1)} %up_ref.1, ...), custom_call_target="tpu_custom_call" | custom-call | tf_op jit(solution)/shard_map/prep/pallas_call | solution.py:208
  19.6 2.7 %collective-permute-start.3 = (bf16[4,16,2048]{2,1,0:T(8,128)(2,1)}, bf16[4,16,2048]{2,1,0:T(8,128)(2,1)S(1)}, u32[]{:S(2)}, u32[]{:S(2)}) collective-permute-start(bf16[4,16,2048]{2,1,0:T(8,128)(2,1)} %get-tuple-element.17.refs_1_.refs_2_.refs_4_.refs_6_), channel_id=1, source_target_pairs={{1,0},{2,1},{3,2},{4,3},{5,4},{6,5},{7,6},{8,7},{9,8},{10,9},{11,1... | collective-permute-start | bytes 786440 | tf_op jit(solution)/shard_map/ppermute | solution.py:489
  22.3 3.1 %collective-permute-start.2 = (bf16[4,16,2048]{2,1,0:T(8,128)(2,1)}, bf16[4,16,2048]{2,1,0:T(8,128)(2,1)S(1)}, u32[]{:S(2)}, u32[]{:S(2)}) collective-permute-start(bf16[4,16,2048]{2,1,0:T(8,128)(2,1)} %get-tuple-element.17.refs_1_.refs_2_.refs_4_.refs_6_), channel_id=1, source_target_pairs={{0,1},{1,2},{2,3},{3,4},{4,5},{5,6},{6,7},{7,8},{8,9},{9,10},{10,1... | collective-permute-start | bytes 786440 | tf_op jit(solution)/shard_map/ppermute | solution.py:489
  25.5 0.0 all-gather.5.cloned.1.call-update
  25.5 0.0 all-gather.7.cloned.1.call-start
  25.5 9.0 %near_early.2.refs_7_ = f32[4,64,2048]{2,1,0:T(8,128)} custom-call(s32[8,17]{1,0:T(8,128)} %get-tuple-element.21.table, bf16[4,64,2048]{2,1,0:T(8,128)(2,1)} %refs_1_.3, bf16[4,16,2048]{2,1,0:T(8,128)(2,1)} %get-tuple-element.17.refs_1_.refs_2_.refs_4_.refs_6_, bf16[4,16,2048]{2,1,0:T(8,128)(2,1)} %get-tuple-element.17.refs_1_.refs_2_.refs_4_.refs_6_), custom_call_target="tpu_custom_call" | custom-call | flops 1024 | bytes 1024 | tf_op jit(solution)/shard_map/near_early/pallas_call | solution.py:295
  34.5 4.6 %collective-permute-done.3.refs_5_ = bf16[4,16,2048]{2,1,0:T(8,128)(2,1)S(1)} collective-permute-done((bf16[4,16,2048]{2,1,0:T(8,128)(2,1)}, bf16[4,16,2048]{2,1,0:T(8,128)(2,1)S(1)}, u32[]{:S(2)}, u32[]{:S(2)}) %collective-permute-start.3) | collective-permute-done | bytes 262176 | tf_op jit(solution)/shard_map/ppermute | solution.py:489
  39.1 0.0 copy-start.1
  39.2 2.7 %collective-permute-done.2.refs_3_ = bf16[4,16,2048]{2,1,0:T(8,128)(2,1)S(1)} collective-permute-done((bf16[4,16,2048]{2,1,0:T(8,128)(2,1)}, bf16[4,16,2048]{2,1,0:T(8,128)(2,1)S(1)}, u32[]{:S(2)}, u32[]{:S(2)}) %collective-permute-start.2) | collective-permute-done | bytes 262176 | tf_op jit(solution)/shard_map/ppermute | solution.py:489
  41.9 0.0 copy-start.2
  41.9 0.0 collective-permute-done.1.refs_2_
  41.9 0.0 copy-start
  41.9 0.0 collective-permute-done.refs_0_
  41.9 0.0 copy-done.1
  41.9 0.7 copy-done.2
  42.6 0.4 copy-done
  42.9 25.0 %near_early.3.refs_8_ = f32[4,64,2048]{2,1,0:T(8,128)} custom-call(s32[8,17]{1,0:T(8,128)} %get-tuple-element.21.table, bf16[4,64,2048]{2,1,0:T(8,128)(2,1)} %collective-permute-done.refs_0_, bf16[4,64,2048]{2,1,0:T(8,128)(2,1)} %refs_1_.3, bf16[4,64,2048]{2,1,0:T(8,128)(2,1)} %copy-done, bf16[4,16,2048]{2,1,0:T(8,128)(2,1)} %copy-done.2, ...), custom_call_target="tpu_custom_call" | custom-call | flops 1099511627776 | bytes 268435456 | tf_op jit(solution)/shard_map/near_early/pallas_call | solution.py:295
  68.0 4.3 %all-gather.5.cloned.1.call-done = bf16[2304,256]{1,0:T(8,128)(2,1)} async-done(((bf16[144,256]{1,0:T(8,128)(2,1)}), bf16[2304,256]{1,0:T(8,128)(2,1)}) %all-gather.5.cloned.1.call-update) | async-done | bytes 1179664 | tf_op jit(solution)/shard_map/all_gather | solution.py:490
  72.3 2.3 %group_pass.1 = bf16[256,256]{1,0:T(8,128)(2,1)} custom-call(s32[1]{0:T(128)} %bitcast.place_ref.group_at_ref, s32[8,256]{1,0:T(8,128)} %skel_ref.1, bf16[16,144,256]{2,1,0:T(8,128)(2,1)} %bitcast.5), custom_call_target="tpu_custom_call" | custom-call | tf_op jit(solution)/shard_map/group_pass/pallas_call | solution.py:377
  74.6 0.0 all-gather.7.cloned.1.call-update
  74.6 39.8 %near_last.1.near_ref = f32[4,64,2048]{2,1,0:T(8,128)} custom-call(s32[8,17]{1,0:T(8,128)} %get-tuple-element.21.table, bf16[4,64,2048]{2,1,0:T(8,128)(2,1)} %collective-permute-done.refs_0_, bf16[4,64,2048]{2,1,0:T(8,128)(2,1)} %refs_1_.3, bf16[4,64,2048]{2,1,0:T(8,128)(2,1)} %copy-done, bf16[4,16,2048]{2,1,0:T(8,128)(2,1)} %copy-done.2, ...), custom_call_target="tpu_custom_call" | custom-call | flops 1024 | bytes 1024 | tf_op jit(solution)/shard_map/near_last/pallas_call | solution.py:345
  114.5 0.0 all-gather.7.cloned.1.call-done
  114.5 8.6 %down_pass.1 = bf16[4,64,2048]{2,1,0:T(8,128)(2,1)} custom-call(s32[1]{0:T(128)} %bitcast.place_ref.group_at_ref, s32[1]{0:T(128)} %bitcast.1.node_at_ref, s32[1,8]{1,0:T(1,128)} %list_ref.1, bf16[16,144,256]{2,1,0:T(8,128)(2,1)} %bitcast.6, bf16[8,256,256]{2,1,0:T(8,128)(2,1)} %bitcast.7, bf16[1,256,256]{2,1,0:T(8,128)(2,1)} %node_transfer_ref.3, ...), custom_call_target="tpu_custom_call" | custom-call | tf_op jit(solution)/shard_map/down_pass/pallas_call | solution.py:437
Async XLA Ops:
  6.5 65.7 %all-gather.5.cloned.1.call-start = ((), (), s32[]{:S(2)}) async-start(), calls=%async_computation | async-start | bytes 1253376 | tf_op jit(solution)/shard_map/all_gather | solution.py:490
  6.5 35.4 %collective-permute-start.1 = (bf16[4,64,2048]{2,1,0:T(8,128)(2,1)}, bf16[4,64,2048]{2,1,0:T(8,128)(2,1)S(1)}, u32[]{:S(2)}, u32[]{:S(2)}) collective-permute-start(bf16[4,64,2048]{2,1,0:T(8,128)(2,1)} %refs_1_.3), channel_id=1, source_target_pairs={{1,0},{2,1},{3,2},{4,3},{5,4},{6,5},{7,6},{8,7},{9,8},{10,9},{11,1... | collective-permute-start | bytes 3145736 | tf_op jit(solution)/shard_map/ppermute | solution.py:485
  9.0 32.9 %collective-permute-start = (bf16[4,64,2048]{2,1,0:T(8,128)(2,1)}, bf16[4,64,2048]{2,1,0:T(8,128)(2,1)}, u32[]{:S(2)}, u32[]{:S(2)}) collective-permute-start(bf16[4,64,2048]{2,1,0:T(8,128)(2,1)} %refs_1_.3), channel_id=1, source_target_pairs={{0,1},{1,2},{2,3},{3,4},{4,5},{5,6},{6,7},{7,8},{8,9},{9,10},{10,1... | collective-permute-start | bytes 3145736 | tf_op jit(solution)/shard_map/ppermute | solution.py:485
  19.6 19.5 %collective-permute-start.3 = (bf16[4,16,2048]{2,1,0:T(8,128)(2,1)}, bf16[4,16,2048]{2,1,0:T(8,128)(2,1)S(1)}, u32[]{:S(2)}, u32[]{:S(2)}) collective-permute-start(bf16[4,16,2048]{2,1,0:T(8,128)(2,1)} %get-tuple-element.17.refs_1_.refs_2_.refs_4_.refs_6_), channel_id=1, source_target_pairs={{1,0},{2,1},{3,2},{4,3},{5,4},{6,5},{7,6},{8,7},{9,8},{10,9},{11,1... | collective-permute-start | bytes 786440 | tf_op jit(solution)/shard_map/ppermute | solution.py:489
  22.3 19.6 %collective-permute-start.2 = (bf16[4,16,2048]{2,1,0:T(8,128)(2,1)}, bf16[4,16,2048]{2,1,0:T(8,128)(2,1)S(1)}, u32[]{:S(2)}, u32[]{:S(2)}) collective-permute-start(bf16[4,16,2048]{2,1,0:T(8,128)(2,1)} %get-tuple-element.17.refs_1_.refs_2_.refs_4_.refs_6_), channel_id=1, source_target_pairs={{0,1},{1,2},{2,3},{3,4},{4,5},{5,6},{6,7},{7,8},{8,9},{9,10},{10,1... | collective-permute-start | bytes 786440 | tf_op jit(solution)/shard_map/ppermute | solution.py:489
  25.5 89.0 %all-gather.7.cloned.1.call-start = ((), (), s32[]{:S(2)}) async-start(), calls=%async_computation.1 | async-start | bytes 1179648 | tf_op jit(solution)/shard_map/all_gather | solution.py:498
  39.1 2.8 %copy-start.1 = (bf16[4,16,2048]{2,1,0:T(8,128)(2,1)}, bf16[4,16,2048]{2,1,0:T(8,128)(2,1)S(1)}, u32[]{:S(2)}) copy-start(bf16[4,16,2048]{2,1,0:T(8,128)(2,1)S(1)} %collective-permute-done.3.refs_5_) | copy-start | bytes 786436
  41.9 0.7 copy-start.2
  41.9 1.1 copy-start
Sparse Core Ops, SparseCore 0:
  25.6 46.6 all-gather.4
  74.8 29.0 all-gather.6

commit v3 on v2

--- a/solution.py
+++ b/solution.py
@@ -20,10 +20,10 @@
 TILE_ROWS = 512
 TILE_COLS = 256
 OWN_UNITS = 4
-LATE_UNITS = 4
+LATE_UNITS = 5
 GROUP_ROWS = 256
 LAST_AT = OWN_UNITS + LATE_UNITS
-LAST_UNITS = 9
+LAST_UNITS = 8
 COLUMNS = LAST_AT + LAST_UNITS
 SIDE, BOX, LIVE, OPENS, CLOSES, PREV, OWN, NEXT = range(8)
 
@@ -118,6 +118,10 @@
     zero = i32(0)
     own_rank = zero
     rest_rank = zero
+    own_count = zero
+    for _, live, side, _ in units:
+        own_count = own_count + (live & (side == 1)).astype(i32)
+    late_limit = jnp.where(own_count >= OWN_UNITS, LATE_UNITS - 2, jnp.where(own_count == OWN_UNITS - 1, LATE_UNITS - 1, LATE_UNITS))
     last_column = i32(LAST_AT)
     own_hold, late_hold, last_hold = [zero] * 3, [zero] * 3, [zero] * 3
     for box in range(boxes):
@@ -127,7 +131,7 @@
             own_hold = put(own_rank, early, box, side, index, own_hold)
             own_rank = own_rank + early.astype(i32)
             rest = live & jnp.logical_not(early)
-            late = rest & (rest_rank < LATE_UNITS)
+            late = rest & (rest_rank < late_limit)
             late_hold = put(OWN_UNITS + rest_rank, late, box, side, index, late_hold)
             rest_rank = rest_rank + rest.astype(i32)
             last = rest & jnp.logical_not(late)

time: 130 us -> 129 us (level)
  the two profiles are of different devices: /device:TPU:66 before, /device:TPU:15 now
where the time goes in v3:
time: 129 us; the launch traced here: 131 us
  Pallas kernels  91.5 us (71%)
  starting transfers between devices  14.8 us (11%)
  between operations  13.5 us (10%)
  waiting for transfers between devices  9.93 us (8%)
    pallas_call x1, Pallas kernels, near_last(): pl.pallas_call(functools.partial(last_kernel, sides), grid_spec=pltpu.Pre...  39.3 us
    pallas_call x2, Pallas kernels, near_early(): pl.pallas_call(functools.partial(early_kernel, start, sides), grid_spec=p...  34.2 us
    pallas_call x1, Pallas kernels, down_pass(): pl.pallas_call(down_kernel, grid=(boxes,), in_specs=[SMEM, SMEM, SMEM, wh...  8.56 us
    ppermute x1, waiting for transfers between devices, shards(): lax.ppermute(pair, 'ty', backward)  8.19 us
    pallas_call x1, Pallas kernels, prep(): pl.pallas_call(prep_kernel, grid=(boxes,), in_specs=[SMEM, SMEM, by_box((...  7.22 us
    ppermute x1, starting transfers between devices, shards(): lax.ppermute(pair, 'ty', forward)  5.47 us
    ppermute x1, starting transfers between devices, shards(): lax.ppermute(probes, 'ty', forward)  4.94 us
  transfers between devices with their start and end apart: 6, of which 3 were waited for; matrix products, arithmetic and copies ran while one was open for 0% of the time, Pallas kernels for 62%

profile of v3, /device:TPU:15, one launch (start us, length us, event | category | flops | bytes accessed | tf_op | source)
XLA Modules:
  0.0 130.8 jit_solution(13887187735909268727)
XLA Ops:
  6.5 0.0 all-gather.5.cloned.1.call-start
  6.5 2.4 %collective-permute-start.1 = (bf16[4,64,2048]{2,1,0:T(8,128)(2,1)}, bf16[4,64,2048]{2,1,0:T(8,128)(2,1)S(1)}, u32[]{:S(2)}, u32[]{:S(2)}) collective-permute-start(bf16[4,64,2048]{2,1,0:T(8,128)(2,1)} %refs_1_.3), channel_id=1, source_target_pairs={{1,0},{2,1},{3,2},{4,3},{5,4},{6,5},{7,6},{8,7},{9,8},{10,9},{11,1... | collective-permute-start | bytes 3145736 | tf_op jit(solution)/shard_map/ppermute | solution.py:489
  9.0 4.9 %collective-permute-start = (bf16[4,64,2048]{2,1,0:T(8,128)(2,1)}, bf16[4,64,2048]{2,1,0:T(8,128)(2,1)}, u32[]{:S(2)}, u32[]{:S(2)}) collective-permute-start(bf16[4,64,2048]{2,1,0:T(8,128)(2,1)} %refs_1_.3), channel_id=1, source_target_pairs={{0,1},{1,2},{2,3},{3,4},{4,5},{5,6},{6,7},{7,8},{8,9},{9,10},{10,1... | collective-permute-start | bytes 3145736 | tf_op jit(solution)/shard_map/ppermute | solution.py:489
  13.9 7.2 %prep.1 = (bf16[4,16,2048]{2,1,0:T(8,128)(2,1)}, s32[8,17]{1,0:T(8,128)}, bf16[144,256]{1,0:T(8,128)(2,1)}) custom-call(s32[4,3]{1,0:T(4,128)} %near_ref.1, s32[1]{0:T(128)} %bitcast.2.base_ref, bf16[4,64,2048]{2,1,0:T(8,128)(2,1)} %refs_1_.3, f32[4,8,2048]{2,1,0:T(8,128)} %points_ref.1, bf16[4,256,2048]{2,1,0:T(8,128)(2,1)} %up_ref.1, ...), custom_call_target="tpu_custom_call" | custom-call | tf_op jit(solution)/shard_map/prep/pallas_call | solution.py:212
  21.2 1.9 %collective-permute-start.3 = (bf16[4,16,2048]{2,1,0:T(8,128)(2,1)}, bf16[4,16,2048]{2,1,0:T(8,128)(2,1)S(1)}, u32[]{:S(2)}, u32[]{:S(2)}) collective-permute-start(bf16[4,16,2048]{2,1,0:T(8,128)(2,1)} %get-tuple-element.17.refs_1_.refs_2_.refs_4_.refs_6_), channel_id=1, source_target_pairs={{1,0},{2,1},{3,2},{4,3},{5,4},{6,5},{7,6},{8,7},{9,8},{10,9},{11,1... | collective-permute-start | bytes 786440 | tf_op jit(solution)/shard_map/ppermute | solution.py:493
  23.1 5.5 %collective-permute-start.2 = (bf16[4,16,2048]{2,1,0:T(8,128)(2,1)}, bf16[4,16,2048]{2,1,0:T(8,128)(2,1)S(1)}, u32[]{:S(2)}, u32[]{:S(2)}) collective-permute-start(bf16[4,16,2048]{2,1,0:T(8,128)(2,1)} %get-tuple-element.17.refs_1_.refs_2_.refs_4_.refs_6_), channel_id=1, source_target_pairs={{0,1},{1,2},{2,3},{3,4},{4,5},{5,6},{6,7},{7,8},{8,9},{9,10},{10,1... | collective-permute-start | bytes 786440 | tf_op jit(solution)/shard_map/ppermute | solution.py:493
  28.6 0.0 all-gather.5.cloned.1.call-update
  28.6 0.0 all-gather.7.cloned.1.call-start
  28.7 3.5 %near_early.2.refs_7_ = f32[4,64,2048]{2,1,0:T(8,128)} custom-call(s32[8,17]{1,0:T(8,128)} %get-tuple-element.21.table, bf16[4,64,2048]{2,1,0:T(8,128)(2,1)} %refs_1_.3, bf16[4,16,2048]{2,1,0:T(8,128)(2,1)} %get-tuple-element.17.refs_1_.refs_2_.refs_4_.refs_6_, bf16[4,16,2048]{2,1,0:T(8,128)(2,1)} %get-tuple-element.17.refs_1_.refs_2_.refs_4_.refs_6_), custom_call_target="tpu_custom_call" | custom-call | flops 1024 | bytes 1024 | tf_op jit(solution)/shard_map/near_early/pallas_call | solution.py:299
  32.2 8.2 %collective-permute-done.3.refs_5_ = bf16[4,16,2048]{2,1,0:T(8,128)(2,1)S(1)} collective-permute-done((bf16[4,16,2048]{2,1,0:T(8,128)(2,1)}, bf16[4,16,2048]{2,1,0:T(8,128)(2,1)S(1)}, u32[]{:S(2)}, u32[]{:S(2)}) %collective-permute-start.3) | collective-permute-done | bytes 262176 | tf_op jit(solution)/shard_map/ppermute | solution.py:493
  40.4 0.0 copy-start.1
  40.4 1.0 collective-permute-done.2.refs_3_
  41.4 0.0 copy-start.2
  41.4 0.0 collective-permute-done.1.refs_2_
  41.4 0.0 copy-start
  41.4 0.0 collective-permute-done.refs_0_
  41.4 0.0 copy-done.1
  41.4 0.7 copy-done.2
  42.1 0.4 copy-done
  42.4 30.6 %near_early.3.refs_8_ = f32[5,64,2048]{2,1,0:T(8,128)} custom-call(s32[8,17]{1,0:T(8,128)} %get-tuple-element.21.table, bf16[4,64,2048]{2,1,0:T(8,128)(2,1)} %collective-permute-done.refs_0_, bf16[4,64,2048]{2,1,0:T(8,128)(2,1)} %refs_1_.3, bf16[4,64,2048]{2,1,0:T(8,128)(2,1)} %copy-done, bf16[4,16,2048]{2,1,0:T(8,128)(2,1)} %copy-done.2, ...), custom_call_target="tpu_custom_call" | custom-call | flops 1099511627776 | bytes 268435456 | tf_op jit(solution)/shard_map/near_early/pallas_call | solution.py:299
  73.0 0.7 all-gather.5.cloned.1.call-done
  73.8 2.3 %group_pass.1 = bf16[256,256]{1,0:T(8,128)(2,1)} custom-call(s32[1]{0:T(128)} %bitcast.place_ref.group_at_ref, s32[8,256]{1,0:T(8,128)} %skel_ref.1, bf16[16,144,256]{2,1,0:T(8,128)(2,1)} %bitcast.5), custom_call_target="tpu_custom_call" | custom-call | tf_op jit(solution)/shard_map/group_pass/pallas_call | solution.py:381
  76.1 0.0 all-gather.7.cloned.1.call-update
  76.1 39.3 %near_last.1.near_ref = f32[4,64,2048]{2,1,0:T(8,128)} custom-call(s32[8,17]{1,0:T(8,128)} %get-tuple-element.21.table, bf16[4,64,2048]{2,1,0:T(8,128)(2,1)} %collective-permute-done.refs_0_, bf16[4,64,2048]{2,1,0:T(8,128)(2,1)} %refs_1_.3, bf16[4,64,2048]{2,1,0:T(8,128)(2,1)} %copy-done, bf16[4,16,2048]{2,1,0:T(8,128)(2,1)} %copy-done.2, ...), custom_call_target="tpu_custom_call" | custom-call | flops 1024 | bytes 1024 | tf_op jit(solution)/shard_map/near_last/pallas_call | solution.py:349
  115.4 0.0 all-gather.7.cloned.1.call-done
  115.4 8.6 %down_pass.1 = bf16[4,64,2048]{2,1,0:T(8,128)(2,1)} custom-call(s32[1]{0:T(128)} %bitcast.place_ref.group_at_ref, s32[1]{0:T(128)} %bitcast.1.node_at_ref, s32[1,8]{1,0:T(1,128)} %list_ref.1, bf16[16,144,256]{2,1,0:T(8,128)(2,1)} %bitcast.6, bf16[8,256,256]{2,1,0:T(8,128)(2,1)} %bitcast.7, bf16[1,256,256]{2,1,0:T(8,128)(2,1)} %node_transfer_ref.3, ...), custom_call_target="tpu_custom_call" | custom-call | tf_op jit(solution)/shard_map/down_pass/pallas_call | solution.py:441
Async XLA Ops:
  6.5 67.2 %all-gather.5.cloned.1.call-start = ((), (), s32[]{:S(2)}) async-start(), calls=%async_computation | async-start | bytes 1253376 | tf_op jit(solution)/shard_map/all_gather | solution.py:494
  6.5 34.8 %collective-permute-start.1 = (bf16[4,64,2048]{2,1,0:T(8,128)(2,1)}, bf16[4,64,2048]{2,1,0:T(8,128)(2,1)S(1)}, u32[]{:S(2)}, u32[]{:S(2)}) collective-permute-start(bf16[4,64,2048]{2,1,0:T(8,128)(2,1)} %refs_1_.3), channel_id=1, source_target_pairs={{1,0},{2,1},{3,2},{4,3},{5,4},{6,5},{7,6},{8,7},{9,8},{10,9},{11,1... | collective-permute-start | bytes 3145736 | tf_op jit(solution)/shard_map/ppermute | solution.py:489
  9.0 32.4 %collective-permute-start = (bf16[4,64,2048]{2,1,0:T(8,128)(2,1)}, bf16[4,64,2048]{2,1,0:T(8,128)(2,1)}, u32[]{:S(2)}, u32[]{:S(2)}) collective-permute-start(bf16[4,64,2048]{2,1,0:T(8,128)(2,1)} %refs_1_.3), channel_id=1, source_target_pairs={{0,1},{1,2},{2,3},{3,4},{4,5},{5,6},{6,7},{7,8},{8,9},{9,10},{10,1... | collective-permute-start | bytes 3145736 | tf_op jit(solution)/shard_map/ppermute | solution.py:489
  21.2 19.2 %collective-permute-start.3 = (bf16[4,16,2048]{2,1,0:T(8,128)(2,1)}, bf16[4,16,2048]{2,1,0:T(8,128)(2,1)S(1)}, u32[]{:S(2)}, u32[]{:S(2)}) collective-permute-start(bf16[4,16,2048]{2,1,0:T(8,128)(2,1)} %get-tuple-element.17.refs_1_.refs_2_.refs_4_.refs_6_), channel_id=1, source_target_pairs={{1,0},{2,1},{3,2},{4,3},{5,4},{6,5},{7,6},{8,7},{9,8},{10,9},{11,1... | collective-permute-start | bytes 786440 | tf_op jit(solution)/shard_map/ppermute | solution.py:493
  23.1 18.3 %collective-permute-start.2 = (bf16[4,16,2048]{2,1,0:T(8,128)(2,1)}, bf16[4,16,2048]{2,1,0:T(8,128)(2,1)S(1)}, u32[]{:S(2)}, u32[]{:S(2)}) collective-permute-start(bf16[4,16,2048]{2,1,0:T(8,128)(2,1)} %get-tuple-element.17.refs_1_.refs_2_.refs_4_.refs_6_), channel_id=1, source_target_pairs={{0,1},{1,2},{2,3},{3,4},{4,5},{5,6},{6,7},{7,8},{8,9},{9,10},{10,1... | collective-permute-start | bytes 786440 | tf_op jit(solution)/shard_map/ppermute | solution.py:493
  28.6 86.8 %all-gather.7.cloned.1.call-start = ((), (), s32[]{:S(2)}) async-start(), calls=%async_computation.1 | async-start | bytes 1179648 | tf_op jit(solution)/shard_map/all_gather | solution.py:502
  40.4 1.0 copy-start.1
  41.4 0.7 copy-start.2
  41.4 1.1 copy-start
Sparse Core Ops, SparseCore 0:
  28.7 44.9 all-gather.4
  76.2 25.6 all-gather.6
